TPU v7x, 32 devices: a whole 2x2x4 slice. The times are simulated.
32 devices in a mesh: row: 8 (over y, x, core), col: 4 (over z).
Axes of the slice: x: 2, y: 2, z: 4, core: 2. Of those that a mesh axis runs over, the one named last changes fastest.
Arguments:
- tokens: bfloat16 [512, 8192], P('row', 'col'), may hold values from -6 to 6
- gate_up: bfloat16 [8192, 2, 16384], P('col', None, 'row'), may hold values from -0.0625 to 0.0625
- cotangent: bfloat16 [512, 16384], P('col', 'row'), may hold values from -6 to 6
Outputs:
- hidden: bfloat16 [512, 16384], P('col', 'row')
- input_grad: bfloat16 [512, 8192], P('row', 'col')
- weight_grad: bfloat16 [8192, 2, 16384], P('col', None, 'row')
All inputs are finite; a program needn't handle non-finite values.
Results may differ from a plain program's by a relative error of at most 0.0049.
Values may be sent and summed in bfloat16 or wider, within the bound.
A program may use at most 128 MiB of HBM per device.

v0:
```python
import jax
import jax.numpy as jnp
from jax import lax
from jax.sharding import PartitionSpec as P


def on_device(tokens, gate_up, cotangent):
    local_feats = tokens.shape[1]
    local_hidden = gate_up.shape[2]
    gathered = lax.all_gather(tokens, "row", axis=0, tiled=True)
    total_rows = gathered.shape[0]
    weights = gate_up.reshape(local_feats, 2 * local_hidden)
    fragment = gathered
    combined = lax.psum_scatter(
        jnp.dot(fragment, weights, preferred_element_type=jnp.float32),
        "col",
        scatter_dimension=0,
        tiled=True,
    )
    gate_pre = combined[:, :local_hidden]
    up_pre = combined[:, local_hidden:]
    sigmoid = jax.nn.sigmoid(gate_pre)
    activated = gate_pre * sigmoid
    hidden = (activated * up_pre).astype(jnp.bfloat16)
    grad_out = cotangent.astype(jnp.float32)
    grad_gate = grad_out * up_pre * sigmoid * (1.0 + gate_pre * (1.0 - sigmoid))
    grad_up = grad_out * activated
    stacked = jnp.stack([grad_gate, grad_up], axis=1).astype(jnp.bfloat16)
    all_grads = lax.all_gather(stacked, "col", axis=0, tiled=True).reshape(
        total_rows, 2 * local_hidden
    )
    weight_grad = lax.dot_general(
        gathered, all_grads, (((0,), (0,)), ((), ())), preferred_element_type=jnp.float32
    )
    weight_grad = weight_grad.astype(jnp.bfloat16).reshape(local_feats, 2, local_hidden)
    fragment = all_grads
    input_grad = lax.psum_scatter(
        lax.dot_general(
            fragment, weights, (((1,), (1,)), ((), ())), preferred_element_type=jnp.float32
        ),
        "row",
        scatter_dimension=0,
        tiled=True,
    ).astype(jnp.bfloat16)
    return (hidden, input_grad, weight_grad)


def solution(mesh):
    in_specs = (P("row", "col"), P("col", None, "row"), P("col", "row"))
    out_specs = (P("col", "row"), P("row", "col"), P("col", None, "row"))
    return jax.shard_map(
        on_device, mesh=mesh, in_specs=in_specs, out_specs=out_specs, check_vma=False
    )
```

profile of v0, /device:TPU:0, one launch (start us, length us, event | category | flops | bytes accessed | tf_op | source)
XLA Modules:
  0.0 381.7 jit_solution(13472984547436944930)
XLA Ops:
  7.2 0.0 all-gather.3.cloned.1.call-start
  7.2 0.7 all-gather.3.cloned.1.call-update
  7.9 0.0 reduce-scatter.3.cloned.1.call-start
  7.9 17.3 %copy.11 = bf16[256,8,2,2048]{3,1,2,0:T(8,128)(2,1)} copy(bf16[256,8,2,2048]{3,2,1,0:T(2,128)(2,1)} %bitcast.17) | data formatting | bytes 33554432
  25.3 15.2 %all-gather.3.cloned.1.call-done = bf16[512,2048]{1,0:T(8,128)(2,1)} async-done(((bf16[64,2048]{1,0:T(8,128)(2,1)}), bf16[512,2048]{1,0:T(8,128)(2,1)}) %all-gather.3.cloned.1.call-update) | async-done | bytes 2097168 | tf_op jit(solution)/shard_map/all_gather | solution.py:10
  40.5 14.9 %fusion.12 = f32[512,4096]{1,0:T(8,128)} fusion(bf16[512,2048]{1,0:T(8,128)(2,1)} %all-gather.3.cloned.1.call-done, bf16[2048,4096]{1,0:T(8,128)(2,1)} %bitcast.18), kind=kOutput, calls=%fused_computation.16 | convolution fusion | flops 8589934592 | bytes 27262976 | tf_op jit(solution)/shard_map/dot_general | solution.py:15
  55.4 0.0 copy-start
  55.4 0.0 reduce-scatter.3.cloned.1.call-update
  55.4 0.0 all-gather.5.cloned.1.call-start
  55.5 144.6 %reduce-scatter.3.cloned.1.call-done = f32[128,4096]{1,0:T(8,128)} async-done(((f32[512,4096]{1,0:T(8,128)}), f32[128,4096]{1,0:T(8,128)}) %reduce-scatter.3.cloned.1.call-update) | async-done | bytes 2097168 | tf_op jit(solution)/shard_map/reduce_scatter | solution.py:14
  200.1 0.0 copy-done
  200.1 3.0 fusion.11
  203.1 1.1 pad_maximum_fusion
  204.1 0.0 all-gather.5.cloned.1.call-update
  204.1 0.2 reduce-scatter.5.cloned.1.call-start
  204.4 81.4 %all-gather.5.cloned.1.call-done = bf16[512,2,2048]{2,0,1:T(8,128)(2,1)} async-done(((bf16[128,2,2048]{2,0,1:T(8,128)(2,1)}), bf16[512,2,2048]{2,0,1:T(8,128)(2,1)}) %all-gather.5.cloned.1.call-update) | async-done | bytes 4194320 | tf_op jit(solution)/shard_map/all_gather | solution.py:29
  285.8 24.4 %fusion.2 = f32[512,2048]{1,0:T(8,128)} fusion(bf16[512,2,2048]{2,0,1:T(8,128)(2,1)} %all-gather.5.cloned.1.call-done, bf16[2048,2,2048]{2,1,0:T(2,128)(2,1)} %param.4), kind=kOutput, calls=%fused_computation.3 | convolution fusion | flops 8589934592 | bytes 25165824 | tf_op jit(solution)/shard_map/dot_general | solution.py:38
  310.1 0.0 reduce-scatter.5.cloned.1.call-update
  310.2 0.0 copy-start.1
  310.2 6.4 %copy.9 = bf16[512,2,2048]{0,2,1:T(8,128)(2,1)} copy(bf16[512,2,2048]{2,0,1:T(8,128)(2,1)} %all-gather.5.cloned.1.call-done) | data formatting | bytes 8388608 | tf_op jit(solution)/shard_map/all_gather | solution.py:29
  316.5 0.0 copy-done.1
  316.5 15.2 %convolution_convert_fusion = bf16[4096,2048]{1,0:T(8,128)(2,1)} fusion(bf16[512,4096]{0,1:T(8,128)(2,1)} %bitcast.20, bf16[512,2048]{1,0:T(8,128)(2,1)S(1)} %copy-done.1), kind=kOutput, calls=%fused_computation.2 | convolution fusion | flops 8598323200 | bytes 23068672 | tf_op jit(solution)/shard_map/dot_general | solution.py:32
  331.7 41.7 %copy.10 = bf16[2048,2,2048]{2,1,0:T(2,128)(2,1)} copy(bf16[2048,2,2048]{0,2,1:T(8,128)(2,1)} %bitcast.19) | data formatting | bytes 33554432
  373.4 0.0 reduce-scatter.5.cloned.1.call-done
  373.4 1.8 convert_element_type.18
Async XLA Ops:
  7.2 33.4 %all-gather.3.cloned.1.call-start = ((), (), s32[]{:S(2)}) async-start(), calls=%async_computation.2 | async-start | bytes 2359296 | tf_op jit(solution)/shard_map/all_gather | solution.py:10
  7.9 192.2 %reduce-scatter.3.cloned.1.call-start = ((), (), s32[]{:S(2)}) async-start(), calls=%async_computation.3 | async-start | bytes 10485760 | tf_op jit(solution)/shard_map/reduce_scatter | solution.py:14
  55.4 144.7 %copy-start = (bf16[128,2048]{1,0:T(8,128)(2,1)S(1)}, bf16[128,2048]{1,0:T(8,128)(2,1)}, u32[]{:S(2)}) copy-start(bf16[128,2048]{1,0:T(8,128)(2,1)} %param.5) | copy-start | bytes 1572868
  55.4 230.3 %all-gather.5.cloned.1.call-start = ((), (), s32[]{:S(2)}) async-start(), calls=%async_computation.4 | async-start | bytes 5242880 | tf_op jit(solution)/shard_map/all_gather | solution.py:29
  204.1 169.2 %reduce-scatter.5.cloned.1.call-start = ((), (), s32[]{:S(2)}) async-start(), calls=%async_computation.5 | async-start | bytes 4718592 | tf_op jit(solution)/shard_map/reduce_scatter | solution.py:37
  310.2 6.4 %copy-start.1 = (bf16[512,2048]{1,0:T(8,128)(2,1)S(1)}, bf16[512,2048]{1,0:T(8,128)(2,1)}, u32[]{:S(2)}) copy-start(bf16[512,2048]{1,0:T(8,128)(2,1)} %all-gather.3.cloned.1.call-done) | copy-start | bytes 6291460
Sparse Core Ops, SparseCore 0:
  9.9 30.5 all-gather.2
  55.6 144.4 reduce-scatter.2
  204.3 81.4 all-gather.4
  310.3 49.8 reduce-scatter.4
where the time goes:
time: 383 us; the launch traced here: 382 us
  waiting for transfers between devices  242 us (63%)
  local copies, waits for them, and re-layouts  65.4 us (17%)
  matrix products  54.4 us (14%)
  between operations  13.8 us (4%)
  other arithmetic  5.8 us (2%)
    reduce_scatter x1, waiting for transfers between devices, on_device(): lax.psum_scatter(jnp.dot(fragment, weights, preferred_element_type=jnp.fl...  145 us
    all_gather x1, waiting for transfers between devices, on_device(): lax.all_gather(stacked, 'col', axis=0, tiled=True)  81.4 us
    unnamed x6, local copies, waits for them, and re-layouts  59 us
    dot_general x1, matrix products, on_device(): lax.dot_general(fragment, weights, (((1,), (1,)), ((), ())), preferred_el...  24.4 us
    all_gather x1, waiting for transfers between devices, on_device(): gathered = lax.all_gather(tokens, 'row', axis=0, tiled=True)  15.2 us
    dot_general x1, matrix products, on_device(): lax.dot_general(gathered, all_grads, (((0,), (0,)), ((), ())), preferred_...  15.2 us
    dot_general x1, matrix products, on_device(): jnp.dot(fragment, weights, preferred_element_type=jnp.float32)  14.9 us
  transfers between devices with their start and end apart: 4, of which 3 were waited for; matrix products, arithmetic and copies ran while one was open for 21% of the time, Pallas kernels for 0%

commit v1 on v0

v1 whole, which is shorter than its diff:
```python
import functools

import jax
import jax.numpy as jnp
from jax import lax
from jax.experimental import pallas as pl
from jax.experimental.pallas import tpu as pltpu
from jax.sharding import PartitionSpec as P

MESH = pl.DeviceIdType.MESH


def exchange_kernel(
    n, width, part_ref, cot_ref, hid_ref, g_ref, from_left, from_right, acc,
    rs_send_r, rs_recv_r, rs_send_l, rs_recv_l, ag_send_r, ag_send_l, ag_recv,
):
    p = lax.axis_index("col")
    rows = cot_ref.shape[0]
    hidden = cot_ref.shape[1]
    chunks = hidden // width
    has_left, has_right = p > 0, p < n - 1

    def place(c, b):
        return (
            slice(None),
            pl.ds(pl.multiple_of(b * rows, rows), rows),
            pl.ds(pl.multiple_of(c * width, width), width),
        )

    def own_part(c, b, k):
        return part_ref[
            pl.ds(pl.multiple_of(b * rows, rows), rows),
            pl.ds(pl.multiple_of(k * hidden + c * width, width), width),
        ]

    def copy(src, dst, send, recv, target):
        return pltpu.make_async_remote_copy(
            src_ref=src, dst_ref=dst, send_sem=send, recv_sem=recv,
            device_id={"col": target}, device_id_type=MESH,
        )

    def rs_right(c, b):
        at = from_left.at[place(c, b)]
        return copy(at, at, rs_send_r.at[c, b], rs_recv_r.at[c, b], p + 1)

    def rs_left(c, b):
        at = from_right.at[place(c, b)]
        return copy(at, at, rs_send_l.at[c, b], rs_recv_l.at[c, b], p - 1)

    def ag_right(c, b):
        at = g_ref.at[place(c, b)]
        return copy(at, at, ag_send_r.at[c, b], ag_recv.at[c, b], p + 1)

    def ag_left(c, b):
        at = g_ref.at[place(c, b)]
        return copy(at, at, ag_send_l.at[c, b], ag_recv.at[c, b], p - 1)

    def relay(c, b, buffer, descriptor, arrives):
        _, at_rows, at_cols = place(c, b)

        @pl.when(arrives)
        def _():
            descriptor(c, b).wait_recv()
            for k in range(2):
                total = own_part(c, b, k) + buffer[k, at_rows, at_cols].astype(jnp.float32)
                buffer[k, at_rows, at_cols] = total.astype(buffer.dtype)

        @pl.when(jnp.logical_not(arrives))
        def _():
            for k in range(2):
                buffer[k, at_rows, at_cols] = own_part(c, b, k).astype(buffer.dtype)

        descriptor(c, b).start()

    def relay_right(c):
        for b in range(n - 1, 0, -1):
            pl.when(p < b)(functools.partial(relay, c, b, from_left, rs_right, has_left))

    def relay_left(c):
        for b in range(n - 1):
            pl.when(p > b)(functools.partial(relay, c, b, from_right, rs_left, has_right))

    def reduce(c):
        @pl.when(2 * p < n)
        def _():
            relay_right(c)
            relay_left(c)

        @pl.when(2 * p >= n)
        def _():
            relay_left(c)
            relay_right(c)

    def finish(c):
        _, at_rows, at_cols = place(c, p)
        for k in range(2):
            acc[k] = own_part(c, p, k)

        @pl.when(has_left)
        def _():
            rs_right(c, p).wait_recv()
            for k in range(2):
                acc[k] += from_left[k, at_rows, at_cols].astype(jnp.float32)

        @pl.when(has_right)
        def _():
            rs_left(c, p).wait_recv()
            for k in range(2):
                acc[k] += from_right[k, at_rows, at_cols].astype(jnp.float32)

        gate_pre, up_pre = acc[0], acc[1]
        sigmoid = jax.nn.sigmoid(gate_pre)
        activated = gate_pre * sigmoid
        grad_out = cot_ref[:, at_cols].astype(jnp.float32)
        hid_ref[:, at_cols] = (activated * up_pre).astype(hid_ref.dtype)
        grad_gate = grad_out * up_pre * sigmoid * (1.0 + gate_pre * (1.0 - sigmoid))
        g_ref[0, at_rows, at_cols] = grad_gate.astype(g_ref.dtype)
        g_ref[1, at_rows, at_cols] = (grad_out * activated).astype(g_ref.dtype)

        @pl.when(has_right)
        def _():
            ag_right(c, p).start()

        @pl.when(has_left)
        def _():
            ag_left(c, p).start()

    def spread(c):
        for d in range(1, n):

            @pl.when(p >= d)
            def _():
                ag_right(c, p - d).wait_recv()

                @pl.when(has_right)
                def _():
                    ag_right(c, p - d).start()

            @pl.when(p + d < n)
            def _():
                ag_left(c, p + d).wait_recv()

                @pl.when(has_left)
                def _():
                    ag_left(c, p + d).start()

    barrier = pltpu.get_barrier_semaphore()
    for here, step in ((has_left, -1), (has_right, 1)):

        @pl.when(here)
        def _():
            pl.semaphore_signal(barrier, inc=1, device_id={"col": p + step}, device_id_type=MESH)

    pl.semaphore_wait(barrier, has_left.astype(jnp.int32) + has_right.astype(jnp.int32))

    def step(i, carry):
        pl.when(i < chunks)(lambda: reduce(i))
        pl.when(jnp.logical_and(i >= 1, i < chunks + 1))(lambda: finish(i - 1))
        pl.when(i >= 2)(lambda: spread(i - 2))
        return carry

    lax.fori_loop(0, chunks + 2, step, 0)

    def drain(c, carry):
        for b in range(n):
            pl.when(p < b)(lambda: rs_right(c, b).wait_send())
            pl.when(p > b)(lambda: rs_left(c, b).wait_send())
            pl.when(jnp.logical_and(has_right, p >= b))(lambda: ag_right(c, b).wait_send())
            pl.when(jnp.logical_and(has_left, p <= b))(lambda: ag_left(c, b).wait_send())
        return carry

    lax.fori_loop(0, chunks, drain, 0)


def exchange(part, cotangent, n):
    rows, hidden = cotangent.shape
    total_rows = part.shape[0]
    width = min(256, hidden)
    chunks = hidden // width
    vmem = pl.BlockSpec(memory_space=pltpu.VMEM)
    sem = pltpu.SemaphoreType.DMA((chunks, n))
    held = pltpu.VMEM((2, total_rows, hidden), jnp.bfloat16)
    return pl.pallas_call(
        functools.partial(exchange_kernel, n, width),
        out_shape=(
            jax.ShapeDtypeStruct((rows, hidden), jnp.bfloat16),
            jax.ShapeDtypeStruct((2, total_rows, hidden), jnp.bfloat16),
        ),
        in_specs=[vmem, vmem],
        out_specs=(vmem, vmem),
        scratch_shapes=[held, held, pltpu.VMEM((2, rows, width), jnp.float32)] + [sem] * 7,
        compiler_params=pltpu.CompilerParams(
            collective_id=0, has_side_effects=True, vmem_limit_bytes=48 * 2**20
        ),
    )(part, cotangent)


def on_device(n_col, tokens, gate_up, cotangent):
    local_feats = tokens.shape[1]
    local_hidden = gate_up.shape[2]
    gathered = lax.all_gather(tokens, "row", axis=0, tiled=True)
    weights = gate_up.reshape(local_feats, 2 * local_hidden)
    part = jnp.dot(gathered, weights, preferred_element_type=jnp.float32)
    hidden, grads = exchange(part, cotangent, n_col)
    flat = jnp.concatenate([grads[0], grads[1]], axis=1)
    input_grad = lax.psum_scatter(
        lax.dot_general(
            flat, weights, (((1,), (1,)), ((), ())), preferred_element_type=jnp.float32
        ),
        "row",
        scatter_dimension=0,
        tiled=True,
    ).astype(jnp.bfloat16)
    weight_grad = jnp.stack(
        [
            lax.dot_general(
                gathered, grads[k], (((0,), (0,)), ((), ())), preferred_element_type=jnp.float32
            ).astype(jnp.bfloat16)
            for k in range(2)
        ],
        axis=1,
    )
    return (hidden, input_grad, weight_grad)


def solution(mesh):
    in_specs = (P("row", "col"), P("col", None, "row"), P("col", "row"))
    out_specs = (P("col", "row"), P("row", "col"), P("col", None, "row"))
    return jax.shard_map(
        functools.partial(on_device, mesh.shape["col"]),
        mesh=mesh, in_specs=in_specs, out_specs=out_specs, check_vma=False,
    )
```

time: 383 us -> 305 us (0.80)
  waiting for transfers between devices: 242 us -> 15.9 us
  Pallas kernels: 0 us -> 161 us
  matrix products: 54.4 us -> 40.2 us
    pallas_call x0 -> x1, Pallas kernels: none -> 161 us  [exchange(): pl.pallas_call(functools.partial(exchange_kernel, n, width), out_shape=(j...]
    reduce_scatter x2 -> x1, waiting for transfers between devices: 145 us -> 0.01 us  [on_device(): lax.psum_scatter(lax.dot_general(flat, weights, (((1,), (1,)), ((), ())),...]
    all_gather x1 -> x0, waiting for transfers between devices: 81.4 us -> none  [on_device(): lax.all_gather(stacked, 'col', axis=0, tiled=True)]
    dot_general x3 -> x4, matrix products: 54.4 us -> 40.2 us  [the longest x1 15 us: on_device(): part = jnp.dot(gathered, weights, preferred_element_type=jnp.float32)]
    all_gather x1 -> x0, local copies, waits for them, and re-layouts: 6.37 us -> none  [on_device(): lax.all_gather(stacked, 'col', axis=0, tiled=True)]
    unnamed x6 -> x11, local copies, waits for them, and re-layouts: 59 us -> 63 us
  transfers between devices with their start and end apart: 4 -> 2, of which waited for: 3 -> 1; matrix products, arithmetic and copies ran while one was open for 21% -> 25% of each run, Pallas kernels for 0% -> 0%
where the time goes in v1:
time: 305 us; the launch traced here: 304 us
  Pallas kernels  161 us (53%)
  local copies, waits for them, and re-layouts  63.3 us (21%)
  matrix products  40.2 us (13%)
  waiting for transfers between devices  15.9 us (5%)
  between operations  14.1 us (5%)
  other arithmetic  8.54 us (3%)
    pallas_call x1, Pallas kernels, exchange(): pl.pallas_call(functools.partial(exchange_kernel, n, width), out_shape=(j...  161 us
    unnamed x11, local copies, waits for them, and re-layouts  63 us
    all_gather x1, waiting for transfers between devices, on_device(): gathered = lax.all_gather(tokens, 'row', axis=0, tiled=True)  15.2 us
    dot_general x1, matrix products, on_device(): part = jnp.dot(gathered, weights, preferred_element_type=jnp.float32)  15 us
    dot_general x1, matrix products, on_device(): lax.dot_general(flat, weights, (((1,), (1,)), ((), ())), preferred_elemen...  13.8 us
    dot_general x2, matrix products, on_device(): lax.dot_general(gathered, grads[k], (((0,), (0,)), ((), ())), preferred_e...  11.4 us
    another operation x1, other arithmetic, on_device(): jnp.stack([lax.dot_general(gathered, grads[k], (((0,), (0,)), ((), ())),...  6.77 us
  transfers between devices with their start and end apart: 2, of which 1 were waited for; matrix products, arithmetic and copies ran while one was open for 25% of the time, Pallas kernels for 0%

profile of v1, /device:TPU:0, one launch (start us, length us, event | category | flops | bytes accessed | tf_op | source)
XLA Modules:
  0.0 303.5 jit_solution(5546031039325809580)
XLA Ops:
  7.2 0.0 all-gather.2.cloned.1.call-start
  7.2 0.7 all-gather.2.cloned.1.call-update
  7.9 0.0 reduce-scatter.2.cloned.1.call-start
  7.9 17.4 %copy.7 = bf16[256,8,2,2048]{3,1,2,0:T(8,128)(2,1)} copy(bf16[256,8,2,2048]{3,2,1,0:T(2,128)(2,1)} %bitcast.21) | data formatting | bytes 33554432
  25.3 15.2 %all-gather.2.cloned.1.call-done = bf16[512,2048]{1,0:T(8,128)(2,1)} async-done(((bf16[64,2048]{1,0:T(8,128)(2,1)}), bf16[512,2048]{1,0:T(8,128)(2,1)}) %all-gather.2.cloned.1.call-update) | async-done | bytes 2097168 | tf_op jit(solution)/shard_map/all_gather | solution.py:201
  40.5 0.0 copy-start.2
  40.5 15.0 %fusion.5.part_ref = f32[512,4096]{1,0:T(8,128)} fusion(bf16[512,2048]{1,0:T(8,128)(2,1)} %all-gather.2.cloned.1.call-done, bf16[2048,4096]{1,0:T(8,128)(2,1)} %bitcast.22), kind=kOutput, calls=%fused_computation.10 | convolution fusion | flops 8589934592 | bytes 27262976 | tf_op jit(solution)/shard_map/dot_general | solution.py:203
  55.5 0.0 copy-done.2
  55.5 161.4 %shard_map.58 = (bf16[128,2048]{1,0:T(8,128)(2,1)S(1)}, bf16[2,512,2048]{2,1,0:T(8,128)(2,1)S(1)}) custom-call(f32[512,4096]{1,0:T(8,128)} %fusion.5.part_ref, bf16[128,2048]{1,0:T(8,128)(2,1)S(1)} %copy-done.2), custom_call_target="tpu_custom_call" | custom-call | tf_op jit(solution)/shard_map/pallas_call | solution.py:183
  216.9 0.0 copy-start
  216.9 0.3 slice_bitcast_fusion.1
  217.2 1.6 copy-done
  218.8 13.8 %fusion = f32[512,2048]{1,0:T(8,128)} fusion(bf16[2048,4096]{1,0:T(8,128)(2,1)} %bitcast.23, bf16[512,2048]{1,0:T(8,128)(2,1)S(1)} %get-tuple-element.11, bf16[512,2048]{1,0:T(8,128)(2,1)S(1)} %get-tuple-element.10), kind=kOutput, calls=%fused_computation.3 | convolution fusion | flops 8598323200 | bytes 25165824 | tf_op jit(solution)/shard_map/dot_general | solution.py:207
  232.7 0.0 copy-start.3
  232.7 0.0 reduce-scatter.2.cloned.1.call-update
  232.7 1.6 copy-done.3
  234.2 0.0 copy-start.1
  234.3 6.6 %convert_bitcast_fusion.1 = bf16[2048,1,2048]{0,2,1:T(8,128)(2,1)S(1)} fusion(bf16[512,2048]{1,0:T(8,128)(2,1)S(1)} %copy-done.3, bf16[2,512,2048]{2,1,0:T(8,128)(2,1)} %copy-done), kind=kOutput, calls=%fused_computation.2 | convolution fusion | flops 4299161600 | bytes 12582912 | tf_op jit(solution)/shard_map/dot_general | solution.py:216
  240.8 0.0 copy-done.1
  240.8 4.8 %convert_bitcast_fusion = bf16[2048,1,2048]{0,2,1:T(8,128)(2,1)S(1)} fusion(bf16[512,2048]{1,0:T(8,128)(2,1)S(1)} %copy-done.3, bf16[2,512,2048]{2,1,0:T(8,128)(2,1)S(1)} %copy-done.1), kind=kOutput, calls=%fused_computation.1 | convolution fusion | flops 4299161600 | bytes 12582912 | tf_op jit(solution)/shard_map/dot_general | solution.py:216
  245.7 6.8 %pad_maximum_fusion = bf16[2048,2,2048]{0,2,1:T(8,128)(2,1)} fusion(bf16[2048,1,2048]{0,2,1:T(8,128)(2,1)S(1)} %convert_bitcast_fusion, bf16[2048,1,2048]{0,2,1:T(8,128)(2,1)S(1)} %convert_bitcast_fusion.1), kind=kLoop, calls=%fused_computation | loop fusion | flops 8388608 | bytes 33554432 | tf_op jit(solution)/shard_map/stack | solution.py:214
  252.5 41.7 %copy.6 = bf16[2048,2,2048]{2,1,0:T(2,128)(2,1)} copy(bf16[2048,2,2048]{0,2,1:T(8,128)(2,1)} %pad_maximum_fusion) | data formatting | bytes 33554432
  294.1 0.0 reduce-scatter.2.cloned.1.call-done
  294.1 1.8 convert_element_type.15
  295.9 0.8 copy.9
Async XLA Ops:
  7.2 33.4 %all-gather.2.cloned.1.call-start = ((), (), s32[]{:S(2)}) async-start(), calls=%async_computation.1 | async-start | bytes 2359296 | tf_op jit(solution)/shard_map/all_gather | solution.py:201
  7.9 286.2 %reduce-scatter.2.cloned.1.call-start = ((), (), s32[]{:S(2)}) async-start(), calls=%async_computation.2 | async-start | bytes 4718592 | tf_op jit(solution)/shard_map/reduce_scatter | solution.py:206
  40.5 15.0 %copy-start.2 = (bf16[128,2048]{1,0:T(8,128)(2,1)S(1)}, bf16[128,2048]{1,0:T(8,128)(2,1)}, u32[]{:S(2)}) copy-start(bf16[128,2048]{1,0:T(8,128)(2,1)} %cot_ref.1) | copy-start | bytes 1572868
  216.9 1.9 copy-start
  232.7 1.6 copy-start.3
  234.2 6.6 %copy-start.1 = (bf16[2,512,2048]{2,1,0:T(8,128)(2,1)S(1)}, bf16[2,512,2048]{2,1,0:T(8,128)(2,1)}, u32[]{:S(2)}) copy-start(bf16[2,512,2048]{2,1,0:T(8,128)(2,1)} %copy-done) | copy-start | bytes 12582916
Sparse Core Ops, SparseCore 0:
  9.9 30.5 all-gather.1
  232.8 49.7 reduce-scatter.1

commit v2 on v0

v2 whole, which is shorter than its diff:
```python
import functools

import jax
import jax.numpy as jnp
from jax import lax
from jax.experimental import pallas as pl
from jax.experimental.pallas import tpu as pltpu
from jax.sharding import PartitionSpec as P

MESH = pl.DeviceIdType.MESH


def exchange_kernel(
    n, unit_rows, width, part_ref, cot_ref, hid_ref, g_ref, from_left, from_right, acc,
    rs_send_r, rs_recv_r, rs_send_l, rs_recv_l, ag_send_r, ag_send_l, ag_recv,
):
    p = lax.axis_index("col")
    rows, hidden = cot_ref.shape
    cuts = rows // unit_rows
    units = cuts * (hidden // width)
    has_left, has_right = p > 0, p < n - 1

    def rows_of(u, b):
        return pl.ds(pl.multiple_of(b * rows + (u % cuts) * unit_rows, unit_rows), unit_rows)

    def cols_of(u, k=0):
        return pl.ds(pl.multiple_of(k * hidden + (u // cuts) * width, width), width)

    def own_part(u, b, k):
        return part_ref[rows_of(u, b), cols_of(u, k)]

    def copy(at, send, recv, target):
        return pltpu.make_async_remote_copy(
            src_ref=at, dst_ref=at, send_sem=send, recv_sem=recv,
            device_id={"col": target}, device_id_type=MESH,
        )

    def rs_right(u, b):
        return copy(from_left.at[u, b], rs_send_r.at[u, b], rs_recv_r.at[u, b], p + 1)

    def rs_left(u, b):
        return copy(from_right.at[u, b], rs_send_l.at[u, b], rs_recv_l.at[u, b], p - 1)

    def ag_right(u, b):
        at = g_ref.at[:, rows_of(u, b), cols_of(u)]
        return copy(at, ag_send_r.at[u, b], ag_recv.at[u, b], p + 1)

    def ag_left(u, b):
        at = g_ref.at[:, rows_of(u, b), cols_of(u)]
        return copy(at, ag_send_l.at[u, b], ag_recv.at[u, b], p - 1)

    def when_unit(u, more, body):
        pl.when(jnp.logical_and(jnp.logical_and(u >= 0, u < units), more))(body)

    def relay(u, b, buffer, descriptor, arrives):
        @pl.when(arrives)
        def _():
            descriptor(u, b).wait_recv()
            for k in range(2):
                total = own_part(u, b, k) + buffer[u, b, k].astype(jnp.float32)
                buffer[u, b, k] = total.astype(buffer.dtype)

        @pl.when(jnp.logical_not(arrives))
        def _():
            for k in range(2):
                buffer[u, b, k] = own_part(u, b, k).astype(buffer.dtype)

        descriptor(u, b).start()

    def finish(u):
        for k in range(2):
            acc[k] = own_part(u, p, k)

        @pl.when(has_left)
        def _():
            rs_right(u, p).wait_recv()
            for k in range(2):
                acc[k] += from_left[u, p, k].astype(jnp.float32)

        @pl.when(has_right)
        def _():
            rs_left(u, p).wait_recv()
            for k in range(2):
                acc[k] += from_right[u, p, k].astype(jnp.float32)

        gate_pre, up_pre = acc[0], acc[1]
        sigmoid = jax.nn.sigmoid(gate_pre)
        activated = gate_pre * sigmoid
        here, at_rows, at_cols = rows_of(u, 0), rows_of(u, p), cols_of(u)
        grad_out = cot_ref[here, at_cols].astype(jnp.float32)
        hid_ref[here, at_cols] = (activated * up_pre).astype(hid_ref.dtype)
        grad_gate = grad_out * up_pre * sigmoid * (1.0 + gate_pre * (1.0 - sigmoid))
        g_ref[0, at_rows, at_cols] = grad_gate.astype(g_ref.dtype)
        g_ref[1, at_rows, at_cols] = (grad_out * activated).astype(g_ref.dtype)

        @pl.when(has_right)
        def _():
            ag_right(u, p).start()

        @pl.when(has_left)
        def _():
            ag_left(u, p).start()

    def forward_right(u, b):
        ag_right(u, b).wait_recv()
        pl.when(has_right)(lambda: ag_right(u, b).start())

    def forward_left(u, b):
        ag_left(u, b).wait_recv()
        pl.when(has_left)(lambda: ag_left(u, b).start())

    barrier = pltpu.get_barrier_semaphore()
    for here, step in ((has_left, -1), (has_right, 1)):

        @pl.when(here)
        def _():
            pl.semaphore_signal(barrier, inc=1, device_id={"col": p + step}, device_id_type=MESH)

    pl.semaphore_wait(barrier, has_left.astype(jnp.int32) + has_right.astype(jnp.int32))

    def iteration(i, carry):
        for s in range(n - 1):
            b = n - 1 - s
            when_unit(
                i - p, p < b,
                functools.partial(relay, i - p, b, from_left, rs_right, has_left),
            )
            when_unit(
                i - (n - 1 - p), p > s,
                functools.partial(relay, i - (n - 1 - p), s, from_right, rs_left, has_right),
            )
        summed = i - jnp.maximum(p, n - 1 - p)
        when_unit(summed, True, functools.partial(finish, summed))
        for b in range(n):
            lag = max(b, n - 1 - b)
            u = i - lag - (p - b)
            when_unit(u, p > b, functools.partial(forward_right, u, b))
            u = i - lag - (b - p)
            when_unit(u, p < b, functools.partial(forward_left, u, b))
        return carry

    lax.fori_loop(0, units + 2 * (n - 1), iteration, 0)

    def drain(u, carry):
        for b in range(n):
            pl.when(p < b)(lambda: rs_right(u, b).wait_send())
            pl.when(p > b)(lambda: rs_left(u, b).wait_send())
            pl.when(jnp.logical_and(has_right, p >= b))(lambda: ag_right(u, b).wait_send())
            pl.when(jnp.logical_and(has_left, p <= b))(lambda: ag_left(u, b).wait_send())
        return carry

    lax.fori_loop(0, units, drain, 0)


def exchange(part, cotangent, n):
    rows, hidden = cotangent.shape
    total_rows = part.shape[0]
    unit_rows, width = 64, 128
    units = (rows // unit_rows) * (hidden // width)
    vmem = pl.BlockSpec(memory_space=pltpu.VMEM)
    sem = pltpu.SemaphoreType.DMA((units, n))
    held = pltpu.VMEM((units, n, 2, unit_rows, width), jnp.bfloat16)
    return pl.pallas_call(
        functools.partial(exchange_kernel, n, unit_rows, width),
        out_shape=(
            jax.ShapeDtypeStruct((rows, hidden), jnp.bfloat16),
            jax.ShapeDtypeStruct((2, total_rows, hidden), jnp.bfloat16),
        ),
        in_specs=[vmem, vmem],
        out_specs=(vmem, vmem),
        scratch_shapes=[held, held, pltpu.VMEM((2, unit_rows, width), jnp.float32)] + [sem] * 7,
        compiler_params=pltpu.CompilerParams(
            collective_id=0, has_side_effects=True, vmem_limit_bytes=48 * 2**20
        ),
    )(part, cotangent)


def tail_kernel(
    n, tile, part_ref, tok_ref, g_ref, in_grad_ref, w_grad_ref, acc, sent, got, tiles,
    send_sem, recv_sem, out_sem,
):
    r = lax.axis_index("row")
    bits = n.bit_length() - 1
    rows, feats = in_grad_ref.shape
    half = feats // 2
    orders = (tuple(range(bits)), (0,) + tuple(range(bits - 1, 0, -1)))

    def own(bit):
        return (r // 2**bit) % 2

    def partner(bit):
        return r + (1 - 2 * own(bit)) * 2**bit

    def block(order, stage, e, keep):
        at = 0
        for bit in order[:stage]:
            at = at + own(bit) * 2**bit
        bit = order[stage]
        at = at + (own(bit) if keep else 1 - own(bit)) * 2**bit
        for place, bit in enumerate(order[stage + 1 :]):
            at = at + ((e >> place) & 1) * 2**bit
        return at

    def slots(stage):
        count = n >> (stage + 1)
        first = n - (n >> stage)
        return [(e, first + e) for e in range(count)]

    def copy(h, stage, slot):
        return pltpu.make_async_remote_copy(
            src_ref=sent.at[h, slot], dst_ref=got.at[h, slot],
            send_sem=send_sem.at[h, slot], recv_sem=recv_sem.at[h, slot],
            device_id={"row": partner(orders[h][stage])}, device_id_type=MESH,
        )

    def send(stage):
        for h in range(2):
            for e, slot in slots(stage):
                b = block(orders[h], stage, e, False)
                value = (part_ref if stage == 0 else acc)[
                    pl.ds(pl.multiple_of(b * rows, rows), rows), h * half : (h + 1) * half
                ]
                sent[h, slot] = value.astype(sent.dtype)
                copy(h, stage, slot).start()

    def receive(stage):
        for h in range(2):
            for e, slot in slots(stage):
                copy(h, stage, slot).wait_recv()
                b = block(orders[h], stage, e, True)
                at = (pl.ds(pl.multiple_of(b * rows, rows), rows), slice(h * half, (h + 1) * half))
                total = (part_ref if stage == 0 else acc)[at] + got[h, slot].astype(jnp.float32)
                if stage == bits - 1:
                    in_grad_ref[:, h * half : (h + 1) * half] = total.astype(in_grad_ref.dtype)
                else:
                    acc[at] = total

    across = feats // tile
    count = 2 * across

    def out_copy(t):
        return pltpu.make_async_copy(
            tiles.at[t % 2],
            w_grad_ref.at[t // across, pl.ds(pl.multiple_of((t % across) * tile, tile), tile)],
            out_sem.at[t % 2],
        )

    def weight_tile(t, carry):
        pl.when(t >= 2)(lambda: out_copy(t - 2).wait())
        cols = pl.ds(pl.multiple_of((t % across) * tile, tile), tile)
        tiles[t % 2] = lax.dot_general(
            tok_ref[:, cols], g_ref[t // across], (((0,), (0,)), ((), ())),
            preferred_element_type=jnp.float32,
        ).astype(tiles.dtype)
        out_copy(t).start()
        return carry

    barrier = pltpu.get_barrier_semaphore()
    for bit in range(bits):
        pl.semaphore_signal(barrier, inc=1, device_id={"row": partner(bit)}, device_id_type=MESH)
    pl.semaphore_wait(barrier, bits)

    shares = 2 * bits - 1
    done = 0
    for stage in range(bits):
        send(stage)
        until = count * (2 * stage + 1) // shares
        lax.fori_loop(done, until, weight_tile, 0)
        done = until
        receive(stage)
    for t in range(count - 2, count):
        out_copy(t).wait()
    for stage in range(bits):
        for h in range(2):
            for _, slot in slots(stage):
                copy(h, stage, slot).wait_send()


def tail(part, gathered, grads, n):
    total_rows, feats = part.shape
    hidden = grads.shape[2]
    rows = total_rows // n
    tile = 256
    vmem = pl.BlockSpec(memory_space=pltpu.VMEM)
    sem = pltpu.SemaphoreType.DMA((2, n - 1))
    held = pltpu.VMEM((2, n - 1, rows, feats // 2), jnp.bfloat16)
    return pl.pallas_call(
        functools.partial(tail_kernel, n, tile),
        out_shape=(
            jax.ShapeDtypeStruct((rows, feats), jnp.bfloat16),
            jax.ShapeDtypeStruct((2, feats, hidden), jnp.bfloat16),
        ),
        in_specs=[vmem, vmem, vmem],
        out_specs=(vmem, pl.BlockSpec(memory_space=pl.ANY)),
        scratch_shapes=[
            pltpu.VMEM((total_rows, feats), jnp.float32), held, held,
            pltpu.VMEM((2, tile, hidden), jnp.bfloat16),
            sem, sem, pltpu.SemaphoreType.DMA((2,)),
        ],
        compiler_params=pltpu.CompilerParams(
            collective_id=1, has_side_effects=True, vmem_limit_bytes=48 * 2**20
        ),
    )(part, gathered, grads)


def on_device(n_row, n_col, tokens, gate_up, cotangent):
    local_feats = tokens.shape[1]
    local_hidden = gate_up.shape[2]
    gathered = lax.all_gather(tokens, "row", axis=0, tiled=True)
    weights = gate_up.reshape(local_feats, 2 * local_hidden)
    part = jnp.dot(gathered, weights, preferred_element_type=jnp.float32)
    hidden, grads = exchange(part, cotangent, n_col)
    flat = jnp.concatenate([grads[0], grads[1]], axis=1)
    in_part = lax.dot_general(
        flat, weights, (((1,), (1,)), ((), ())), preferred_element_type=jnp.float32
    )
    input_grad, weight_grad = tail(in_part, gathered, grads, n_row)
    return (hidden, input_grad, jnp.transpose(weight_grad, (1, 0, 2)))


def solution(mesh):
    in_specs = (P("row", "col"), P("col", None, "row"), P("col", "row"))
    out_specs = (P("col", "row"), P("row", "col"), P("col", None, "row"))
    return jax.shard_map(
        functools.partial(on_device, mesh.shape["row"], mesh.shape["col"]),
        mesh=mesh, in_specs=in_specs, out_specs=out_specs, check_vma=False,
    )
```

time: 383 us -> 258 us (0.67)
  waiting for transfers between devices: 242 us -> 15.9 us
  Pallas kernels: 0 us -> 147 us
  matrix products: 54.4 us -> 29 us
  local copies, waits for them, and re-layouts: 65.4 us -> 51.8 us
  other arithmetic: 5.8 us -> 0 us
    pallas_call x0 -> x2, Pallas kernels: none -> 147 us  [the longest x1 124 us: exchange(): pl.pallas_call(functools.partial(exchange_kernel, n, unit_rows, width), o...]
    reduce_scatter x2 -> x0, waiting for transfers between devices: 145 us -> none  [the longest x1 145 us: on_device(): lax.psum_scatter(jnp.dot(fragment, weights, preferred_element_type=jnp.fl...]
    all_gather x1 -> x0, waiting for transfers between devices: 81.4 us -> none  [on_device(): lax.all_gather(stacked, 'col', axis=0, tiled=True)]
    dot_general x3 -> x2, matrix products: 54.4 us -> 29 us  [the longest x1 15 us: on_device(): part = jnp.dot(gathered, weights, preferred_element_type=jnp.float32)]
    unnamed x6 -> x10, local copies, waits for them, and re-layouts: 59 us -> 51.5 us
    all_gather x1 -> x0, local copies, waits for them, and re-layouts: 6.37 us -> none  [on_device(): lax.all_gather(stacked, 'col', axis=0, tiled=True)]
    another operation x2 -> x0, other arithmetic: 4.03 us -> none  [on_device(): stacked = jnp.stack([grad_gate, grad_up], axis=1).astype(jnp.bfloat16)]
  transfers between devices with their start and end apart: 4 -> 1, of which waited for: 3 -> 1; matrix products, arithmetic and copies ran while one was open for 21% -> 7% of each run, Pallas kernels for 0% -> 0%
where the time goes in v2:
time: 258 us; the launch traced here: 257 us
  Pallas kernels  147 us (57%)
  local copies, waits for them, and re-layouts  51.8 us (20%)
  matrix products  29 us (11%)
  waiting for transfers between devices  15.9 us (6%)
  between operations  14.1 us (5%)
    pallas_call x1, Pallas kernels, exchange(): pl.pallas_call(functools.partial(exchange_kernel, n, unit_rows, width), o...  124 us
    unnamed x10, local copies, waits for them, and re-layouts  51.5 us
    pallas_call x1, Pallas kernels, tail(): pl.pallas_call(functools.partial(tail_kernel, n, tile), out_shape=(jax.Sh...  22 us
    all_gather x1, waiting for transfers between devices, on_device(): gathered = lax.all_gather(tokens, 'row', axis=0, tiled=True)  15.3 us
    dot_general x1, matrix products, on_device(): part = jnp.dot(gathered, weights, preferred_element_type=jnp.float32)  15 us
    dot_general x1, matrix products, on_device(): lax.dot_general(flat, weights, (((1,), (1,)), ((), ())), preferred_elemen...  14 us
  transfers between devices with their start and end apart: 1, of which 1 were waited for; matrix products, arithmetic and copies ran while one was open for 7% of the time, Pallas kernels for 0%

profile of v2, /device:TPU:0, one launch (start us, length us, event | category | flops | bytes accessed | tf_op | source)
XLA Modules:
  0.0 257.4 jit_solution(2893545554767539675)
XLA Ops:
  7.2 0.0 all-gather.2.cloned.1.call-start
  7.2 0.7 all-gather.2.cloned.1.call-update
  7.9 17.3 %copy.7 = bf16[256,8,2,2048]{3,1,2,0:T(8,128)(2,1)} copy(bf16[256,8,2,2048]{3,2,1,0:T(2,128)(2,1)} %bitcast.10) | data formatting | bytes 33554432
  25.2 15.3 %all-gather.2.cloned.1.call-done.tok_ref = bf16[512,2048]{1,0:T(8,128)(2,1)} async-done(((bf16[64,2048]{1,0:T(8,128)(2,1)}), bf16[512,2048]{1,0:T(8,128)(2,1)}) %all-gather.2.cloned.1.call-update) | async-done | bytes 2097168 | tf_op jit(solution)/shard_map/all_gather | solution.py:309
  40.5 0.0 copy-start.2
  40.5 15.0 %fusion.5.part_ref = f32[512,4096]{1,0:T(8,128)} fusion(bf16[512,2048]{1,0:T(8,128)(2,1)} %all-gather.2.cloned.1.call-done.tok_ref, bf16[2048,4096]{1,0:T(8,128)(2,1)} %bitcast.11), kind=kOutput, calls=%fused_computation.7 | convolution fusion | flops 8589934592 | bytes 27262976 | tf_op jit(solution)/shard_map/dot_general | solution.py:311
  55.5 0.0 copy-done.2
  55.5 124.5 %shard_map.58 = (bf16[128,2048]{1,0:T(8,128)(2,1)S(1)}, bf16[2,512,2048]{2,1,0:T(8,128)(2,1)S(1)}) custom-call(f32[512,4096]{1,0:T(8,128)} %fusion.5.part_ref, bf16[128,2048]{1,0:T(8,128)(2,1)S(1)} %copy-done.2), custom_call_target="tpu_custom_call" | custom-call | tf_op jit(solution)/shard_map/pallas_call | solution.py:163
  180.0 0.0 copy-start
  180.1 0.3 slice_bitcast_fusion.1
  180.4 1.7 copy-done
  182.0 0.0 copy-start.1
  182.0 14.0 %fusion.part_ref = f32[512,2048]{1,0:T(8,128)} fusion(bf16[2048,4096]{1,0:T(8,128)(2,1)} %bitcast.12, bf16[512,2048]{1,0:T(8,128)(2,1)S(1)} %get-tuple-element.15, bf16[512,2048]{1,0:T(8,128)(2,1)S(1)} %get-tuple-element.14), kind=kOutput, calls=%fused_computation | convolution fusion | flops 8598323200 | bytes 25165824 | tf_op jit(solution)/shard_map/dot_general | solution.py:314
  196.0 0.0 copy-done.1
  196.0 22.0 %shard_map.59 = (bf16[64,2048]{1,0:T(8,128)(2,1)S(1)}, bf16[2,2048,2048]{2,1,0:T(8,128)(2,1)}) custom-call(f32[512,2048]{1,0:T(8,128)} %fusion.part_ref, bf16[512,2048]{1,0:T(8,128)(2,1)S(1)} %copy-done.1, bf16[2,512,2048]{2,1,0:T(8,128)(2,1)} %copy-done), custom_call_target="tpu_custom_call" | custom-call | tf_op jit(solution)/shard_map/pallas_call | solution.py:287
  218.1 31.0 %copy.6 = bf16[2048,2,2048]{2,1,0:T(2,128)(2,1)} copy(bf16[2048,2,2048]{2,0,1:T(8,128)(2,1)} %bitcast.13) | data formatting | bytes 33554432
  249.0 0.8 copy.10
  249.8 0.7 copy.11
Async XLA Ops:
  7.2 33.4 %all-gather.2.cloned.1.call-start = ((), (), s32[]{:S(2)}) async-start(), calls=%async_computation | async-start | bytes 2359296 | tf_op jit(solution)/shard_map/all_gather | solution.py:309
  40.5 15.0 %copy-start.2 = (bf16[128,2048]{1,0:T(8,128)(2,1)S(1)}, bf16[128,2048]{1,0:T(8,128)(2,1)}, u32[]{:S(2)}) copy-start(bf16[128,2048]{1,0:T(8,128)(2,1)} %cot_ref.1) | copy-start | bytes 1572868
  180.0 2.0 copy-start
  182.0 14.0 %copy-start.1 = (bf16[512,2048]{1,0:T(8,128)(2,1)S(1)}, bf16[512,2048]{1,0:T(8,128)(2,1)}, u32[]{:S(2)}) copy-start(bf16[512,2048]{1,0:T(8,128)(2,1)} %all-gather.2.cloned.1.call-done.tok_ref) | copy-start | bytes 6291460
Sparse Core Ops, SparseCore 0:
  9.9 30.5 all-gather.1

commit v3 on v2

--- a/solution.py
+++ b/solution.py
@@ -4,6 +4,7 @@
 import jax.numpy as jnp
 from jax import lax
 from jax.experimental import pallas as pl
+from jax.experimental.layout import Layout, with_layout_constraint
 from jax.experimental.pallas import tpu as pltpu
 from jax.sharding import PartitionSpec as P
 
@@ -11,13 +12,18 @@
 
 
 def exchange_kernel(
-    n, unit_rows, width, part_ref, cot_ref, hid_ref, g_ref, from_left, from_right, acc,
-    rs_send_r, rs_recv_r, rs_send_l, rs_recv_l, ag_send_r, ag_send_l, ag_recv,
+    n, unit_rows, width, group, tok_ref, w_ref, cot_ref, hid_ref, in_part_ref, w_grad_ref,
+    weights, tok_t, part_ref, g_ref, from_left, from_right, acc, tiles,
+    rs_send_r, rs_recv_r, rs_send_l, rs_recv_l, ag_send_r, ag_send_l, ag_recv, w_sem, out_sem,
 ):
     p = lax.axis_index("col")
     rows, hidden = cot_ref.shape
     cuts = rows // unit_rows
     units = cuts * (hidden // width)
+    total_rows, feats = tok_ref.shape
+    groups, steps = hidden // group, cuts * group // width
+    halves = steps // 2
+    lag_max = 2 * (n - 1)
     has_left, has_right = p > 0, p < n - 1
 
     def rows_of(u, b):
@@ -116,6 +122,73 @@
         def _():
             pl.semaphore_signal(barrier, inc=1, device_id={"col": p + step}, device_id_type=MESH)
 
+    def weight_copy(q, k):
+        return pltpu.make_async_copy(
+            w_ref.at[:, pl.ds(pl.multiple_of(k * hidden + q * group, group), group)],
+            weights.at[q, k], w_sem.at[q, k],
+        )
+
+    def group_cols(q, k=0):
+        return pl.ds(pl.multiple_of(k * hidden + q * group, group), group)
+
+    def piece(j, size):
+        return pl.ds(pl.multiple_of(j * size, size), size)
+
+    def forward_step(q, j):
+        @pl.when(j == 0)
+        def _():
+            weight_copy(q, 0).wait()
+            weight_copy(q, 1).wait()
+
+        k, at = j // halves, piece(j % halves, total_rows // halves)
+        part_ref[at, group_cols(q, k)] = jnp.dot(
+            tok_ref[at, :], weights[q, k], preferred_element_type=jnp.float32
+        )
+
+    def out_copy(t):
+        j = t % steps
+        size = feats // halves // 16
+        return pltpu.make_async_copy(
+            tiles.at[t % 2],
+            w_grad_ref.at[piece(j % halves, size), j // halves, :, group_cols(t // steps)],
+            out_sem.at[t % 2],
+        )
+
+    def backward_step(t):
+        q, j = t // steps, t % steps
+        at = piece(j, total_rows // steps)
+        in_part_ref[at, :] += sum(
+            lax.dot_general(
+                g_ref[k, at, group_cols(q)], weights[q, k], (((1,), (1,)), ((), ())),
+                preferred_element_type=jnp.float32,
+            )
+            for k in range(2)
+        )
+        pl.when(t >= 2)(lambda: out_copy(t - 2).wait())
+        tile = jnp.dot(
+            tok_t[piece(j % halves, feats // halves), :], g_ref[j // halves, :, group_cols(q)],
+            preferred_element_type=jnp.float32,
+        )
+        tiles[t % 2] = tile.astype(tiles.dtype).reshape(tiles.shape[1:])
+        out_copy(t).start()
+
+    for q in range(groups):
+        for k in range(2):
+            weight_copy(q, k).start()
+    in_part_ref[...] = jnp.zeros_like(in_part_ref)
+
+    def turn(j, carry):
+        at = piece(j, group)
+        tok_t[at, :] = tok_ref[:, at].T
+        return carry
+
+    lax.fori_loop(0, feats // group, turn, 0)
+
+    def first(j, carry):
+        forward_step(0, j)
+        return carry
+
+    lax.fori_loop(0, steps, first, 0)
     pl.semaphore_wait(barrier, has_left.astype(jnp.int32) + has_right.astype(jnp.int32))
 
     def iteration(i, carry):
@@ -137,9 +210,13 @@
             when_unit(u, p > b, functools.partial(forward_right, u, b))
             u = i - lag - (b - p)
             when_unit(u, p < b, functools.partial(forward_left, u, b))
+        pl.when(i + steps < units)(lambda: forward_step(i // steps + 1, i % steps))
+        pl.when(i >= lag_max + steps)(lambda: backward_step(i - lag_max - steps))
         return carry
 
-    lax.fori_loop(0, units + 2 * (n - 1), iteration, 0)
+    lax.fori_loop(0, units + lag_max + steps, iteration, 0)
+    for t in range(units - 2, units):
+        out_copy(t).wait()
 
     def drain(u, carry):
         for b in range(n):
@@ -152,33 +229,42 @@
     lax.fori_loop(0, units, drain, 0)
 
 
-def exchange(part, cotangent, n):
+def exchange(gathered, weights, cotangent, n):
     rows, hidden = cotangent.shape
-    total_rows = part.shape[0]
-    unit_rows, width = 64, 128
+    total_rows, feats = gathered.shape
+    unit_rows, width, group = 64, 128, 256
     units = (rows // unit_rows) * (hidden // width)
+    steps = (rows // unit_rows) * (group // width)
     vmem = pl.BlockSpec(memory_space=pltpu.VMEM)
+    hbm = pl.BlockSpec(memory_space=pl.ANY)
     sem = pltpu.SemaphoreType.DMA((units, n))
     held = pltpu.VMEM((units, n, 2, unit_rows, width), jnp.bfloat16)
     return pl.pallas_call(
-        functools.partial(exchange_kernel, n, unit_rows, width),
+        functools.partial(exchange_kernel, n, unit_rows, width, group),
         out_shape=(
             jax.ShapeDtypeStruct((rows, hidden), jnp.bfloat16),
-            jax.ShapeDtypeStruct((2, total_rows, hidden), jnp.bfloat16),
+            jax.ShapeDtypeStruct((total_rows, feats), jnp.float32),
+            jax.ShapeDtypeStruct((feats // 16, 2, 16, hidden), jnp.bfloat16),
         ),
-        in_specs=[vmem, vmem],
-        out_specs=(vmem, vmem),
-        scratch_shapes=[held, held, pltpu.VMEM((2, unit_rows, width), jnp.float32)] + [sem] * 7,
+        in_specs=[vmem, hbm, vmem],
+        out_specs=(vmem, vmem, hbm),
+        scratch_shapes=[
+            pltpu.VMEM((hidden // group, 2, feats, group), jnp.bfloat16),
+            pltpu.VMEM((feats, total_rows), jnp.bfloat16),
+            pltpu.VMEM((total_rows, 2 * hidden), jnp.float32),
+            pltpu.VMEM((2, total_rows, hidden), jnp.bfloat16),
+            held, held, pltpu.VMEM((2, unit_rows, width), jnp.float32),
+            pltpu.VMEM((2, feats * 2 // steps // 16, 16, group), jnp.bfloat16),
+        ]
+        + [sem] * 7
+        + [pltpu.SemaphoreType.DMA((hidden // group, 2)), pltpu.SemaphoreType.DMA((2,))],
         compiler_params=pltpu.CompilerParams(
-            collective_id=0, has_side_effects=True, vmem_limit_bytes=48 * 2**20
+            collective_id=0, has_side_effects=True, vmem_limit_bytes=58 * 2**20
         ),
-    )(part, cotangent)
-
-
-def tail_kernel(
-    n, tile, part_ref, tok_ref, g_ref, in_grad_ref, w_grad_ref, acc, sent, got, tiles,
-    send_sem, recv_sem, out_sem,
-):
+    )(gathered, weights, cotangent)
+
+
+def tail_kernel(n, part_ref, in_grad_ref, acc, sent, got, send_sem, recv_sem):
     r = lax.axis_index("row")
     bits = n.bit_length() - 1
     rows, feats = in_grad_ref.shape
@@ -235,72 +321,36 @@
                 else:
                     acc[at] = total
 
-    across = feats // tile
-    count = 2 * across
-
-    def out_copy(t):
-        return pltpu.make_async_copy(
-            tiles.at[t % 2],
-            w_grad_ref.at[t // across, pl.ds(pl.multiple_of((t % across) * tile, tile), tile)],
-            out_sem.at[t % 2],
-        )
-
-    def weight_tile(t, carry):
-        pl.when(t >= 2)(lambda: out_copy(t - 2).wait())
-        cols = pl.ds(pl.multiple_of((t % across) * tile, tile), tile)
-        tiles[t % 2] = lax.dot_general(
-            tok_ref[:, cols], g_ref[t // across], (((0,), (0,)), ((), ())),
-            preferred_element_type=jnp.float32,
-        ).astype(tiles.dtype)
-        out_copy(t).start()
-        return carry
-
     barrier = pltpu.get_barrier_semaphore()
     for bit in range(bits):
         pl.semaphore_signal(barrier, inc=1, device_id={"row": partner(bit)}, device_id_type=MESH)
     pl.semaphore_wait(barrier, bits)
 
-    shares = 2 * bits - 1
-    done = 0
     for stage in range(bits):
         send(stage)
-        until = count * (2 * stage + 1) // shares
-        lax.fori_loop(done, until, weight_tile, 0)
-        done = until
         receive(stage)
-    for t in range(count - 2, count):
-        out_copy(t).wait()
     for stage in range(bits):
         for h in range(2):
             for _, slot in slots(stage):
                 copy(h, stage, slot).wait_send()
 
 
-def tail(part, gathered, grads, n):
+def tail(part, n):
     total_rows, feats = part.shape
-    hidden = grads.shape[2]
     rows = total_rows // n
-    tile = 256
     vmem = pl.BlockSpec(memory_space=pltpu.VMEM)
     sem = pltpu.SemaphoreType.DMA((2, n - 1))
     held = pltpu.VMEM((2, n - 1, rows, feats // 2), jnp.bfloat16)
     return pl.pallas_call(
-        functools.partial(tail_kernel, n, tile),
-        out_shape=(
-            jax.ShapeDtypeStruct((rows, feats), jnp.bfloat16),
-            jax.ShapeDtypeStruct((2, feats, hidden), jnp.bfloat16),
-        ),
-        in_specs=[vmem, vmem, vmem],
-        out_specs=(vmem, pl.BlockSpec(memory_space=pl.ANY)),
-        scratch_shapes=[
-            pltpu.VMEM((total_rows, feats), jnp.float32), held, held,
-            pltpu.VMEM((2, tile, hidden), jnp.bfloat16),
-            sem, sem, pltpu.SemaphoreType.DMA((2,)),
-        ],
+        functools.partial(tail_kernel, n),
+        out_shape=jax.ShapeDtypeStruct((rows, feats), jnp.bfloat16),
+        in_specs=[vmem],
+        out_specs=vmem,
+        scratch_shapes=[pltpu.VMEM((total_rows, feats), jnp.float32), held, held, sem, sem],
         compiler_params=pltpu.CompilerParams(
             collective_id=1, has_side_effects=True, vmem_limit_bytes=48 * 2**20
         ),
-    )(part, gathered, grads)
+    )(part)
 
 
 def on_device(n_row, n_col, tokens, gate_up, cotangent):
@@ -308,14 +358,13 @@
     local_hidden = gate_up.shape[2]
     gathered = lax.all_gather(tokens, "row", axis=0, tiled=True)
     weights = gate_up.reshape(local_feats, 2 * local_hidden)
-    part = jnp.dot(gathered, weights, preferred_element_type=jnp.float32)
-    hidden, grads = exchange(part, cotangent, n_col)
-    flat = jnp.concatenate([grads[0], grads[1]], axis=1)
-    in_part = lax.dot_general(
-        flat, weights, (((1,), (1,)), ((), ())), preferred_element_type=jnp.float32
+    hidden, in_part, weight_grad = exchange(gathered, weights, cotangent, n_col)
+    input_grad = tail(in_part, n_row)
+    weight_grad = with_layout_constraint(
+        jnp.transpose(weight_grad, (0, 2, 1, 3)), Layout(major_to_minor=(0, 1, 2, 3))
     )
-    input_grad, weight_grad = tail(in_part, gathered, grads, n_row)
-    return (hidden, input_grad, jnp.transpose(weight_grad, (1, 0, 2)))
+    weight_grad = weight_grad.reshape(gate_up.shape)
+    return (hidden, input_grad, weight_grad)
 
 
 def solution(mesh):

time: 258 us -> 241 us (0.934)
  matrix products: 29 us -> 0 us
  Pallas kernels: 147 us -> 159 us
    pallas_call x0 -> x1, local copies, waits for them, and re-layouts: none -> 30.7 us  [exchange(): pl.pallas_call(functools.partial(exchange_kernel, n, unit_rows, width, gr...]
    unnamed x10 -> x7, local copies, waits for them, and re-layouts: 51.5 us -> 21 us
    dot_general x2 -> x0, matrix products: 29 us -> none  [the longest x1 15 us: on_device(): part = jnp.dot(gathered, weights, preferred_element_type=jnp.float32)]
    pallas_call x2, Pallas kernels: 147 us -> 159 us  [the longest x1 143 us: exchange(): pl.pallas_call(functools.partial(exchange_kernel, n, unit_rows, width, gr...]
where the time goes in v3:
time: 241 us
  Pallas kernels  159 us (66%)
  local copies, waits for them, and re-layouts  51.8 us (21%)
  waiting for transfers between devices  15.9 us (7%)
  between operations  14.1 us (6%)
    pallas_call x1, Pallas kernels, exchange(): pl.pallas_call(functools.partial(exchange_kernel, n, unit_rows, width, gr...  143 us
    pallas_call x1, local copies, waits for them, and re-layouts, exchange(): pl.pallas_call(functools.partial(exchange_kernel, n, unit_rows, width, gr...  30.7 us
    unnamed x7, local copies, waits for them, and re-layouts  21 us
    pallas_call x1, Pallas kernels, tail(): pl.pallas_call(functools.partial(tail_kernel, n), out_shape=jax.ShapeDtyp...  16.3 us
    all_gather x1, waiting for transfers between devices, on_device(): gathered = lax.all_gather(tokens, 'row', axis=0, tiled=True)  15.3 us
  transfers between devices with their start and end apart: 1, of which 1 were waited for; matrix products, arithmetic and copies ran while one was open for 7% of the time, Pallas kernels for 0%

profile of v3, /device:TPU:0, one launch (start us, length us, event | category | flops | bytes accessed | tf_op | source)
XLA Modules:
  0.0 240.9 jit_solution(7369193289781381987)
XLA Ops:
  7.2 0.0 all-gather.2.cloned.1.call-start
  7.2 0.7 all-gather.2.cloned.1.call-update
  7.9 17.3 %copy.7 = bf16[256,8,2,2048]{3,1,2,0:T(8,128)(2,1)} copy(bf16[256,8,2,2048]{3,2,1,0:T(2,128)(2,1)} %bitcast.6) | data formatting | bytes 33554432
  25.2 15.3 %all-gather.2.cloned.1.call-done.tok_ref = bf16[512,2048]{1,0:T(8,128)(2,1)} async-done(((bf16[64,2048]{1,0:T(8,128)(2,1)}), bf16[512,2048]{1,0:T(8,128)(2,1)}) %all-gather.2.cloned.1.call-update) | async-done | bytes 2097168 | tf_op jit(solution)/shard_map/all_gather | solution.py:359
  40.5 142.8 %shard_map.58 = (bf16[128,2048]{1,0:T(8,128)(2,1)}, f32[512,2048]{1,0:T(8,128)}, bf16[128,2,16,2048]{3,2,1,0:T(8,128)(2,1)}) custom-call(bf16[512,2048]{1,0:T(8,128)(2,1)} %all-gather.2.cloned.1.call-done.tok_ref, bf16[2048,4096]{1,0:T(8,128)(2,1)} %bitcast.5, bf16[128,2048]{1,0:T(8,128)(2,1)} %cot_ref.1), custom_call_target="tpu_custom_call" | custom-call | tf_op jit(solution)/shard_map/pallas_call | solution.py:242
  183.4 0.0 copy-start
  183.4 2.2 copy-done
  185.6 16.3 %shard_map.59 = bf16[64,2048]{1,0:T(8,128)(2,1)S(1)} custom-call(f32[512,2048]{1,0:T(8,128)S(1)} %copy-done), custom_call_target="tpu_custom_call" | custom-call | tf_op jit(solution)/shard_map/pallas_call | solution.py:344
  201.8 0.0 copy-start.1
  201.8 30.7 %copy.6 = bf16[128,2,16,2048]{3,1,2,0:T(2,128)(2,1)} copy(bf16[128,2,16,2048]{3,2,1,0:T(8,128)(2,1)} %get-tuple-element.8) | data formatting | bytes 33554432 | tf_op jit(solution)/shard_map/pallas_call | solution.py:242
  232.6 0.0 copy-done.1
  232.6 0.8 copy.10
  233.4 0.7 copy.11
Async XLA Ops:
  7.2 33.4 %all-gather.2.cloned.1.call-start = ((), (), s32[]{:S(2)}) async-start(), calls=%async_computation | async-start | bytes 2359296 | tf_op jit(solution)/shard_map/all_gather | solution.py:359
  183.4 2.2 copy-start
  201.8 30.8 %copy-start.1 = (bf16[128,2048]{1,0:T(8,128)(2,1)S(1)}, bf16[128,2048]{1,0:T(8,128)(2,1)}, u32[]{:S(2)}) copy-start(bf16[128,2048]{1,0:T(8,128)(2,1)} %get-tuple-element.12) | copy-start | bytes 1572868
Sparse Core Ops, SparseCore 0:
  9.9 30.5 all-gather.1

commit v4 on v3

--- a/solution.py
+++ b/solution.py
@@ -157,13 +157,22 @@
     def backward_step(t):
         q, j = t // steps, t % steps
         at = piece(j, total_rows // steps)
-        in_part_ref[at, :] += sum(
+        share = sum(
             lax.dot_general(
                 g_ref[k, at, group_cols(q)], weights[q, k], (((1,), (1,)), ((), ())),
                 preferred_element_type=jnp.float32,
             )
             for k in range(2)
         )
+
+        @pl.when(q == 0)
+        def _():
+            in_part_ref[at, :] = share
+
+        @pl.when(q > 0)
+        def _():
+            in_part_ref[at, :] += share
+
         pl.when(t >= 2)(lambda: out_copy(t - 2).wait())
         tile = jnp.dot(
             tok_t[piece(j % halves, feats // halves), :], g_ref[j // halves, :, group_cols(q)],
@@ -172,23 +181,19 @@
         tiles[t % 2] = tile.astype(tiles.dtype).reshape(tiles.shape[1:])
         out_copy(t).start()
 
+    def turn(j):
+        at = piece(j, group)
+        tok_t[at, :] = tok_ref[:, at].T
+
+    def first(j, carry):
+        forward_step(0, j)
+        return carry
+
     for q in range(groups):
         for k in range(2):
             weight_copy(q, k).start()
-    in_part_ref[...] = jnp.zeros_like(in_part_ref)
-
-    def turn(j, carry):
-        at = piece(j, group)
-        tok_t[at, :] = tok_ref[:, at].T
-        return carry
-
-    lax.fori_loop(0, feats // group, turn, 0)
-
-    def first(j, carry):
-        forward_step(0, j)
-        return carry
-
-    lax.fori_loop(0, steps, first, 0)
+        if q == 0:
+            lax.fori_loop(0, steps, first, 0)
     pl.semaphore_wait(barrier, has_left.astype(jnp.int32) + has_right.astype(jnp.int32))
 
     def iteration(i, carry):
@@ -211,9 +216,11 @@
             u = i - lag - (b - p)
             when_unit(u, p < b, functools.partial(forward_left, u, b))
         pl.when(i + steps < units)(lambda: forward_step(i // steps + 1, i % steps))
+        pl.when(i < feats // group)(lambda: turn(i))
         pl.when(i >= lag_max + steps)(lambda: backward_step(i - lag_max - steps))
         return carry
 
+    assert feats // group <= lag_max + steps
     lax.fori_loop(0, units + lag_max + steps, iteration, 0)
     for t in range(units - 2, units):
         out_copy(t).wait()

time: 241 us -> 243 us (level)
  no operation moved by 1% of the time
where the time goes in v4:
time: 243 us
  Pallas kernels  161 us (66%)
  local copies, waits for them, and re-layouts  51.8 us (21%)
  waiting for transfers between devices  15.9 us (7%)
  between operations  14.1 us (6%)
    pallas_call x1, Pallas kernels, exchange(): pl.pallas_call(functools.partial(exchange_kernel, n, unit_rows, width, gr...  144 us
    pallas_call x1, local copies, waits for them, and re-layouts, exchange(): pl.pallas_call(functools.partial(exchange_kernel, n, unit_rows, width, gr...  30.7 us
    unnamed x7, local copies, waits for them, and re-layouts  21 us
    pallas_call x1, Pallas kernels, tail(): pl.pallas_call(functools.partial(tail_kernel, n), out_shape=jax.ShapeDtyp...  16.8 us
    all_gather x1, waiting for transfers between devices, on_device(): gathered = lax.all_gather(tokens, 'row', axis=0, tiled=True)  15.3 us
  transfers between devices with their start and end apart: 1, of which 1 were waited for; matrix products, arithmetic and copies ran while one was open for 7% of the time, Pallas kernels for 0%

profile of v4, /device:TPU:0, one launch (start us, length us, event | category | flops | bytes accessed | tf_op | source)
XLA Modules:
  0.0 242.7 jit_solution(6976551389368251528)
XLA Ops:
  7.2 0.0 all-gather.2.cloned.1.call-start
  7.2 0.7 all-gather.2.cloned.1.call-update
  7.9 17.3 %copy.7 = bf16[256,8,2,2048]{3,1,2,0:T(8,128)(2,1)} copy(bf16[256,8,2,2048]{3,2,1,0:T(2,128)(2,1)} %bitcast.6) | data formatting | bytes 33554432
  25.2 15.3 %all-gather.2.cloned.1.call-done.tok_ref = bf16[512,2048]{1,0:T(8,128)(2,1)} async-done(((bf16[64,2048]{1,0:T(8,128)(2,1)}), bf16[512,2048]{1,0:T(8,128)(2,1)}) %all-gather.2.cloned.1.call-update) | async-done | bytes 2097168 | tf_op jit(solution)/shard_map/all_gather | solution.py:366
  40.5 144.1 %shard_map.58 = (bf16[128,2048]{1,0:T(8,128)(2,1)}, f32[512,2048]{1,0:T(8,128)}, bf16[128,2,16,2048]{3,2,1,0:T(8,128)(2,1)}) custom-call(bf16[512,2048]{1,0:T(8,128)(2,1)} %all-gather.2.cloned.1.call-done.tok_ref, bf16[2048,4096]{1,0:T(8,128)(2,1)} %bitcast.5, bf16[128,2048]{1,0:T(8,128)(2,1)} %cot_ref.1), custom_call_target="tpu_custom_call" | custom-call | tf_op jit(solution)/shard_map/pallas_call | solution.py:249
  184.6 0.0 copy-start
  184.6 2.2 copy-done
  186.8 16.8 %shard_map.59 = bf16[64,2048]{1,0:T(8,128)(2,1)S(1)} custom-call(f32[512,2048]{1,0:T(8,128)S(1)} %copy-done), custom_call_target="tpu_custom_call" | custom-call | tf_op jit(solution)/shard_map/pallas_call | solution.py:351
  203.6 0.0 copy-start.1
  203.6 30.7 %copy.6 = bf16[128,2,16,2048]{3,1,2,0:T(2,128)(2,1)} copy(bf16[128,2,16,2048]{3,2,1,0:T(8,128)(2,1)} %get-tuple-element.8) | data formatting | bytes 33554432 | tf_op jit(solution)/shard_map/pallas_call | solution.py:249
  234.4 0.0 copy-done.1
  234.4 0.8 copy.10
  235.2 0.7 copy.11
Async XLA Ops:
  7.2 33.4 %all-gather.2.cloned.1.call-start = ((), (), s32[]{:S(2)}) async-start(), calls=%async_computation | async-start | bytes 2359296 | tf_op jit(solution)/shard_map/all_gather | solution.py:366
  184.6 2.2 copy-start
  203.6 30.8 %copy-start.1 = (bf16[128,2048]{1,0:T(8,128)(2,1)S(1)}, bf16[128,2048]{1,0:T(8,128)(2,1)}, u32[]{:S(2)}) copy-start(bf16[128,2048]{1,0:T(8,128)(2,1)} %get-tuple-element.12) | copy-start | bytes 1572868
Sparse Core Ops, SparseCore 0:
  9.9 30.5 all-gather.1

commit v5 on v4

--- a/solution.py
+++ b/solution.py
@@ -12,10 +12,14 @@
 
 
 def exchange_kernel(
-    n, unit_rows, width, group, tok_ref, w_ref, cot_ref, hid_ref, in_part_ref, w_grad_ref,
-    weights, tok_t, part_ref, g_ref, from_left, from_right, acc, tiles,
+    n, n_row, unit_rows, width, group, *refs,
+):
+    blocks = refs[:n_row]
+    (
+    w_ref, cot_ref, hid_ref, in_part_ref, w_grad_ref, weights, tok_ref, tok_t, part_ref, g_ref, from_left, from_right, acc, tiles,
     rs_send_r, rs_recv_r, rs_send_l, rs_recv_l, ag_send_r, ag_send_l, ag_recv, w_sem, out_sem,
-):
+    tok_sem,
+    ) = refs[n_row:]
     p = lax.axis_index("col")
     rows, hidden = cot_ref.shape
     cuts = rows // unit_rows
@@ -181,6 +185,20 @@
         tiles[t % 2] = tile.astype(tiles.dtype).reshape(tiles.shape[1:])
         out_copy(t).start()
 
+    r = lax.axis_index("row")
+
+    def block_copy(d):
+        at = 0
+        for bit in range(n_row.bit_length() - 1):
+            mine = (r // 2**bit) % 2
+            at = at + (1 - mine if (d >> bit) & 1 else mine) * 2**bit
+        return pltpu.make_async_copy(
+            blocks[d], tok_ref.at[piece(at, total_rows // n_row)], tok_sem.at[d]
+        )
+
+    for d in range(n_row):
+        block_copy(d).start()
+
     def turn(j):
         at = piece(j, group)
         tok_t[at, :] = tok_ref[:, at].T
@@ -193,6 +211,8 @@
         for k in range(2):
             weight_copy(q, k).start()
         if q == 0:
+            for d in range(n_row):
+                block_copy(d).wait()
             lax.fori_loop(0, steps, first, 0)
     pl.semaphore_wait(barrier, has_left.astype(jnp.int32) + has_right.astype(jnp.int32))
 
@@ -236,9 +256,10 @@
     lax.fori_loop(0, units, drain, 0)
 
 
-def exchange(gathered, weights, cotangent, n):
+def exchange(blocks, weights, cotangent, n):
     rows, hidden = cotangent.shape
-    total_rows, feats = gathered.shape
+    n_row = len(blocks)
+    total_rows, feats = n_row * blocks[0].shape[0], blocks[0].shape[1]
     unit_rows, width, group = 64, 128, 256
     units = (rows // unit_rows) * (hidden // width)
     steps = (rows // unit_rows) * (group // width)
@@ -247,16 +268,17 @@
     sem = pltpu.SemaphoreType.DMA((units, n))
     held = pltpu.VMEM((units, n, 2, unit_rows, width), jnp.bfloat16)
     return pl.pallas_call(
-        functools.partial(exchange_kernel, n, unit_rows, width, group),
+        functools.partial(exchange_kernel, n, n_row, unit_rows, width, group),
         out_shape=(
             jax.ShapeDtypeStruct((rows, hidden), jnp.bfloat16),
             jax.ShapeDtypeStruct((total_rows, feats), jnp.float32),
             jax.ShapeDtypeStruct((feats // 16, 2, 16, hidden), jnp.bfloat16),
         ),
-        in_specs=[vmem, hbm, vmem],
+        in_specs=[hbm] * n_row + [hbm, vmem],
         out_specs=(vmem, vmem, hbm),
         scratch_shapes=[
             pltpu.VMEM((hidden // group, 2, feats, group), jnp.bfloat16),
+            pltpu.VMEM((total_rows, feats), jnp.bfloat16),
             pltpu.VMEM((feats, total_rows), jnp.bfloat16),
             pltpu.VMEM((total_rows, 2 * hidden), jnp.float32),
             pltpu.VMEM((2, total_rows, hidden), jnp.bfloat16),
@@ -264,11 +286,12 @@
             pltpu.VMEM((2, feats * 2 // steps // 16, 16, group), jnp.bfloat16),
         ]
         + [sem] * 7
-        + [pltpu.SemaphoreType.DMA((hidden // group, 2)), pltpu.SemaphoreType.DMA((2,))],
+        + [pltpu.SemaphoreType.DMA((hidden // group, 2)), pltpu.SemaphoreType.DMA((2,))]
+        + [pltpu.SemaphoreType.DMA((n_row,))],
         compiler_params=pltpu.CompilerParams(
             collective_id=0, has_side_effects=True, vmem_limit_bytes=58 * 2**20
         ),
-    )(gathered, weights, cotangent)
+    )(*blocks, weights, cotangent)
 
 
 def tail_kernel(n, part_ref, in_grad_ref, acc, sent, got, send_sem, recv_sem):
@@ -360,12 +383,20 @@
     )(part)
 
 
+def gather_blocks(tokens, n):
+    def swapped(block, d):
+        return lax.ppermute(block, "row", [(i, i ^ d) for i in range(n)])
+
+    even = [tokens] + [swapped(tokens, d) for d in range(2, n, 2)]
+    return [block for d, own in enumerate(even) for block in (own, swapped(own, 1))]
+
+
 def on_device(n_row, n_col, tokens, gate_up, cotangent):
     local_feats = tokens.shape[1]
     local_hidden = gate_up.shape[2]
-    gathered = lax.all_gather(tokens, "row", axis=0, tiled=True)
+    blocks = gather_blocks(tokens, n_row)
     weights = gate_up.reshape(local_feats, 2 * local_hidden)
-    hidden, in_part, weight_grad = exchange(gathered, weights, cotangent, n_col)
+    hidden, in_part, weight_grad = exchange(blocks, weights, cotangent, n_col)
     input_grad = tail(in_part, n_row)
     weight_grad = with_layout_constraint(
         jnp.transpose(weight_grad, (0, 2, 1, 3)), Layout(major_to_minor=(0, 1, 2, 3))

time: 243 us -> 232 us (0.955)
  between operations: 14.1 us -> 0.74 us
  starting transfers between devices: 0.04 us -> 4.59 us
  waiting for transfers between devices: 15.9 us -> 11.8 us
    all_gather x1 -> x0, waiting for transfers between devices: 15.3 us -> none  [on_device(): gathered = lax.all_gather(tokens, 'row', axis=0, tiled=True)]
    ppermute x0 -> x7, waiting for transfers between devices: none -> 11.8 us  [swapped(): return lax.ppermute(block, 'row', [(i, i ^ d) for i in range(n)])]
    ppermute x0 -> x7, starting transfers between devices: none -> 4.59 us  [swapped(): return lax.ppermute(block, 'row', [(i, i ^ d) for i in range(n)])]
    unnamed x7 -> x21, local copies, waits for them, and re-layouts: 21 us -> 22 us
  transfers between devices with their start and end apart: 1 -> 7, of which waited for: 1 -> 3; matrix products, arithmetic and copies ran while one was open for 7% -> 7% of each run, Pallas kernels for 0% -> 0%
where the time goes in v5:
time: 232 us
  Pallas kernels  162 us (70%)
  local copies, waits for them, and re-layouts  52.7 us (23%)
  waiting for transfers between devices  11.8 us (5%)
  starting transfers between devices  4.59 us (2%)
    pallas_call x1, Pallas kernels, exchange(): pl.pallas_call(functools.partial(exchange_kernel, n, n_row, unit_rows, wi...  146 us
    pallas_call x1, local copies, waits for them, and re-layouts, exchange(): pl.pallas_call(functools.partial(exchange_kernel, n, n_row, unit_rows, wi...  30.7 us
    unnamed x21, local copies, waits for them, and re-layouts  22 us
    pallas_call x1, Pallas kernels, tail(): pl.pallas_call(functools.partial(tail_kernel, n), out_shape=jax.ShapeDtyp...  16.6 us
    ppermute x7, waiting for transfers between devices, swapped(): return lax.ppermute(block, 'row', [(i, i ^ d) for i in range(n)])  11.8 us
  transfers between devices with their start and end apart: 7, of which 3 were waited for; matrix products, arithmetic and copies ran while one was open for 7% of the time, Pallas kernels for 0%

profile of v5, /device:TPU:0, one launch (start us, length us, event | category | flops | bytes accessed | tf_op | source)
XLA Modules:
  0.0 232.0 jit_solution(15987696139145581412)
XLA Ops:
  0.6 3.0 %collective-permute-start.3 = (bf16[64,2048]{1,0:T(8,128)(2,1)}, bf16[64,2048]{1,0:T(8,128)(2,1)S(1)}, u32[]{:S(2)}, u32[]{:S(2)}) collective-permute-start(bf16[64,2048]{1,0:T(8,128)(2,1)} %refs_0_.1), channel_id=1, source_target_pairs={{0,16},{4,20},{8,24},{12,28},{16,0},{20,4},{24,8},{28,12},{1,17},{... | collective-permute-start | bytes 786440 | tf_op jit(solution)/shard_map/ppermute | solution.py:388
  3.7 1.5 collective-permute-start.1
  5.2 0.1 collective-permute-start.5
  5.2 0.0 collective-permute-start
  5.2 5.0 %collective-permute-done.3.refs_4_ = bf16[64,2048]{1,0:T(8,128)(2,1)S(1)} collective-permute-done((bf16[64,2048]{1,0:T(8,128)(2,1)}, bf16[64,2048]{1,0:T(8,128)(2,1)S(1)}, u32[]{:S(2)}, u32[]{:S(2)}) %collective-permute-start.3) | collective-permute-done | bytes 262176 | tf_op jit(solution)/shard_map/ppermute | solution.py:388
  10.2 0.0 collective-permute-start.4
  10.2 2.9 %collective-permute-done.1.refs_2_ = bf16[64,2048]{1,0:T(8,128)(2,1)S(1)} collective-permute-done((bf16[64,2048]{1,0:T(8,128)(2,1)}, bf16[64,2048]{1,0:T(8,128)(2,1)S(1)}, u32[]{:S(2)}, u32[]{:S(2)}) %collective-permute-start.1) | collective-permute-done | bytes 262176 | tf_op jit(solution)/shard_map/ppermute | solution.py:388
  13.1 0.0 collective-permute-start.2
  13.1 3.9 %collective-permute-done.5.refs_6_ = bf16[64,2048]{1,0:T(8,128)(2,1)S(1)} collective-permute-done((bf16[64,2048]{1,0:T(8,128)(2,1)}, bf16[64,2048]{1,0:T(8,128)(2,1)S(1)}, u32[]{:S(2)}, u32[]{:S(2)}) %collective-permute-start.5) | collective-permute-done | bytes 262176 | tf_op jit(solution)/shard_map/ppermute | solution.py:388
  17.1 0.0 collective-permute-start.6
  17.1 17.4 %copy.7 = bf16[256,8,2,2048]{3,1,2,0:T(8,128)(2,1)} copy(bf16[256,8,2,2048]{3,2,1,0:T(2,128)(2,1)} %bitcast.6) | data formatting | bytes 33554432
  34.4 0.0 copy-done.2
  34.4 0.0 copy-done.3
  34.4 0.0 copy-done.4
  34.4 0.0 collective-permute-done.refs_1_
  34.4 0.0 copy-start.5
  34.4 0.0 collective-permute-done.4.refs_5_
  34.5 0.0 copy-start.6
  34.5 0.0 collective-permute-done.2.refs_3_
  34.5 0.0 copy-start.7
  34.5 0.0 collective-permute-done.6.refs_7_
  34.5 0.0 copy-start.8
  34.5 0.6 copy-done.5
  35.1 0.1 copy-done.6
  35.2 0.1 copy-done.7
  35.3 0.1 copy-done.8
  35.4 145.6 %shard_map.58 = (bf16[128,2048]{1,0:T(8,128)(2,1)}, f32[512,2048]{1,0:T(8,128)}, bf16[128,2,16,2048]{3,2,1,0:T(8,128)(2,1)}) custom-call(bf16[64,2048]{1,0:T(8,128)(2,1)} %refs_0_.1, bf16[64,2048]{1,0:T(8,128)(2,1)} %copy-done.5, bf16[64,2048]{1,0:T(8,128)(2,1)} %copy-done.3, bf16[64,2048]{1,0:T(8,128)(2,1)} %copy-done.7, bf16[64,2048]{1,0:T(8,128)(2,1)} %copy-done.2, ...), custom_call_target="tpu_custom_call" | custom-call | tf_op jit(solution)/shard_map/pallas_call | solution.py:270
  181.0 2.2 copy-done
  183.2 16.6 %shard_map.59 = bf16[64,2048]{1,0:T(8,128)(2,1)S(1)} custom-call(f32[512,2048]{1,0:T(8,128)S(1)} %copy-done), custom_call_target="tpu_custom_call" | custom-call | tf_op jit(solution)/shard_map/pallas_call | solution.py:374
  199.8 30.7 %copy.6 = bf16[128,2,16,2048]{3,1,2,0:T(2,128)(2,1)} copy(bf16[128,2,16,2048]{3,2,1,0:T(8,128)(2,1)} %get-tuple-element.8) | data formatting | bytes 33554432 | tf_op jit(solution)/shard_map/pallas_call | solution.py:270
  230.5 0.8 copy.10
  231.3 0.7 copy.11
  (6 shorter events, 0.0 us)
Async XLA Ops:
  0.6 9.6 %collective-permute-start.3 = (bf16[64,2048]{1,0:T(8,128)(2,1)}, bf16[64,2048]{1,0:T(8,128)(2,1)S(1)}, u32[]{:S(2)}, u32[]{:S(2)}) collective-permute-start(bf16[64,2048]{1,0:T(8,128)(2,1)} %refs_0_.1), channel_id=1, source_target_pairs={{0,16},{4,20},{8,24},{12,28},{16,0},{20,4},{24,8},{28,12},{1,17},{... | collective-permute-start | bytes 786440 | tf_op jit(solution)/shard_map/ppermute | solution.py:388
  3.7 9.4 %collective-permute-start.1 = (bf16[64,2048]{1,0:T(8,128)(2,1)}, bf16[64,2048]{1,0:T(8,128)(2,1)S(1)}, u32[]{:S(2)}, u32[]{:S(2)}) collective-permute-start(bf16[64,2048]{1,0:T(8,128)(2,1)} %refs_0_.1), channel_id=1, source_target_pairs={{0,8},{4,12},{8,0},{12,4},{16,24},{20,28},{24,16},{28,20},{1,9},{5... | collective-permute-start | bytes 786440 | tf_op jit(solution)/shard_map/ppermute | solution.py:388
  5.2 11.9 %collective-permute-start.5 = (bf16[64,2048]{1,0:T(8,128)(2,1)}, bf16[64,2048]{1,0:T(8,128)(2,1)S(1)}, u32[]{:S(2)}, u32[]{:S(2)}) collective-permute-start(bf16[64,2048]{1,0:T(8,128)(2,1)} %refs_0_.1), channel_id=1, source_target_pairs={{0,24},{4,28},{8,16},{12,20},{16,8},{20,12},{24,0},{28,4},{1,25},{... | collective-permute-start | bytes 786440 | tf_op jit(solution)/shard_map/ppermute | solution.py:388
  5.2 29.2 %collective-permute-start = (bf16[64,2048]{1,0:T(8,128)(2,1)}, bf16[64,2048]{1,0:T(8,128)(2,1)S(1)}, u32[]{:S(2)}, u32[]{:S(2)}) collective-permute-start(bf16[64,2048]{1,0:T(8,128)(2,1)} %refs_0_.1), channel_id=1, source_target_pairs={{0,4},{4,0},{8,12},{12,8},{16,20},{20,16},{24,28},{28,24},{1,5},{5... | collective-permute-start | bytes 786440 | tf_op jit(solution)/shard_map/ppermute | solution.py:388
  10.2 24.2 %copy-start.2 = (bf16[64,2048]{1,0:T(8,128)(2,1)}, bf16[64,2048]{1,0:T(8,128)(2,1)S(1)}, u32[]{:S(2)}) copy-start(bf16[64,2048]{1,0:T(8,128)(2,1)S(1)} %collective-permute-done.3.refs_4_) | copy-start | bytes 786436
  10.2 24.3 %collective-permute-start.4 = (bf16[64,2048]{1,0:T(8,128)(2,1)S(1)}, bf16[64,2048]{1,0:T(8,128)(2,1)S(1)}, u32[]{:S(2)}, u32[]{:S(2)}) collective-permute-start(bf16[64,2048]{1,0:T(8,128)(2,1)S(1)} %collective-permute-done.3.refs_4_), channel_id=1, source_target_pairs={{0,4},{4,0},{8,12},{12,8},{16,20},{20,16},{24,28},{28,24},{1,5},{5... | collective-permute-start | bytes 786440 | tf_op jit(solution)/shard_map/ppermute | solution.py:388
  13.1 21.3 %copy-start.3 = (bf16[64,2048]{1,0:T(8,128)(2,1)}, bf16[64,2048]{1,0:T(8,128)(2,1)S(1)}, u32[]{:S(2)}) copy-start(bf16[64,2048]{1,0:T(8,128)(2,1)S(1)} %collective-permute-done.1.refs_2_) | copy-start | bytes 786436
  13.1 21.4 %collective-permute-start.2 = (bf16[64,2048]{1,0:T(8,128)(2,1)S(1)}, bf16[64,2048]{1,0:T(8,128)(2,1)S(1)}, u32[]{:S(2)}, u32[]{:S(2)}) collective-permute-start(bf16[64,2048]{1,0:T(8,128)(2,1)S(1)} %collective-permute-done.1.refs_2_), channel_id=1, source_target_pairs={{0,4},{4,0},{8,12},{12,8},{16,20},{20,16},{24,28},{28,24},{1,5},{5... | collective-permute-start | bytes 786440 | tf_op jit(solution)/shard_map/ppermute | solution.py:388
  17.1 17.4 %copy-start.4 = (bf16[64,2048]{1,0:T(8,128)(2,1)}, bf16[64,2048]{1,0:T(8,128)(2,1)S(1)}, u32[]{:S(2)}) copy-start(bf16[64,2048]{1,0:T(8,128)(2,1)S(1)} %collective-permute-done.5.refs_6_) | copy-start | bytes 786436
  17.1 17.4 %collective-permute-start.6 = (bf16[64,2048]{1,0:T(8,128)(2,1)S(1)}, bf16[64,2048]{1,0:T(8,128)(2,1)S(1)}, u32[]{:S(2)}, u32[]{:S(2)}) collective-permute-start(bf16[64,2048]{1,0:T(8,128)(2,1)S(1)} %collective-permute-done.5.refs_6_), channel_id=1, source_target_pairs={{0,4},{4,0},{8,12},{12,8},{16,20},{20,16},{24,28},{28,24},{1,5},{5... | collective-permute-start | bytes 786440 | tf_op jit(solution)/shard_map/ppermute | solution.py:388
  34.4 0.7 copy-start.5
  34.5 0.8 copy-start.6
  34.5 0.8 copy-start.7
  34.5 0.9 copy-start.8
  181.0 2.2 copy-start
  199.8 30.8 %copy-start.1 = (bf16[128,2048]{1,0:T(8,128)(2,1)S(1)}, bf16[128,2048]{1,0:T(8,128)(2,1)}, u32[]{:S(2)}) copy-start(bf16[128,2048]{1,0:T(8,128)(2,1)} %get-tuple-element.12) | copy-start | bytes 1572868
